TPU v7x, 32 devices: a whole 2x2x4 slice. The times are simulated.
32 devices in a mesh: aux: 8 (over z, core), pairs: 4 (over y, x).
Axes of the slice: x: 2, y: 2, z: 4, core: 2. Of those that a mesh axis runs over, the one named last changes fastest.
Arguments:
- amplitudes: bfloat16 [8, 256, 256], P(None, 'aux', 'pairs'), may hold values from -6 to 6
- three_index: bfloat16 [224, 256, 256], P('aux'), may hold values from -0.078125 to 0.078125
- virt_energy: float32 [256], replicated, may hold values from 0.2 to 1.5
- pair_energy: float32 [8], replicated, may hold values from -1.5 to -0.3
- owner: int32 [8], replicated, may hold values from 0 to 3, as said below
- partner: int32 [8], replicated, may hold values from 0 to 7, as said below
Outputs:
- blocks: float32 [16, 256, 256], P('pairs', 'aux')
Inputs may be any that keep to these rules, and one draw needn't show every extreme that they name: `owner`: no group index is named by more than 4 pairs, and one group is named by exactly 4 pairs. partner[partner[p]] == p for every pair p.
All inputs are finite; a program needn't handle non-finite values.
Results may differ from a plain program's by a relative error of at most 0.0029.
Values may be sent and summed in bfloat16 or wider, within the bound.
A program may use at most 64 MiB of HBM per device.

v0:
```python
import jax
import jax.numpy as jnp
from jax import lax
from jax.sharding import PartitionSpec as P


def ladder_rows(amp_tiles, three_index):
    whole_tiles = lax.all_gather(amp_tiles, "aux", axis=1, tiled=True)

    def one_slot(slot_tile):
        half_product = jnp.einsum(
            "cd,qbd->qcb", slot_tile, three_index, preferred_element_type=jnp.float32
        ).astype(jnp.bfloat16)
        return jnp.einsum(
            "qac,qcb->ab", three_index, half_product, preferred_element_type=jnp.float32
        )

    running = lax.map(one_slot, whole_tiles)
    return lax.psum_scatter(running, "aux", scatter_dimension=1, tiled=True)


def scale_turn(summed, energies, virt_energy, row_count):
    row_offset = lax.axis_index("aux") * row_count
    virt_rows = lax.dynamic_slice_in_dim(virt_energy, row_offset, row_count)
    divisor = virt_rows[None, :, None] + virt_energy[None, None, :] - energies[:, None, None]
    scaled = summed / divisor
    turned = lax.all_to_all(scaled, "aux", split_axis=2, concat_axis=1, tiled=True)
    return (scaled, jnp.swapaxes(turned, 1, 2))


def per_device(amplitudes, three_index, virt_energy, pair_energy, owner, partner):
    groups = lax.axis_size("pairs")
    my_group = lax.axis_index("pairs")
    pairs_all = owner.shape[0]
    row_count = amplitudes.shape[1]
    per_group = pairs_all // groups
    capacity = 2 * per_group
    pair_ids = jnp.arange(pairs_all, dtype=jnp.int32)
    earlier = (owner[None, :] == owner[:, None]) & (pair_ids[None, :] < pair_ids[:, None])
    position = owner * capacity + jnp.sum(earlier.astype(jnp.int32), axis=1)
    partner_table = partner[:, None] == pair_ids[None, :]
    own_ids = my_group * capacity + jnp.arange(capacity, dtype=jnp.int32)
    own_link = (position[None, :] == own_ids[:, None]).astype(jnp.float32)
    arrived = lax.all_to_all(amplitudes, "pairs", split_axis=0, concat_axis=2, tiled=True)
    summed = ladder_rows(arrived, three_index)
    energies = lax.dynamic_slice_in_dim(pair_energy, my_group * per_group, per_group)
    scaled, flipped = scale_turn(summed, energies, virt_energy, row_count)
    partner_link = jnp.dot(
        own_link, partner_table.astype(jnp.float32), precision=lax.Precision.HIGHEST
    )
    running = jnp.einsum(
        "sp,prb->srb",
        own_link,
        lax.all_gather(scaled, "pairs", axis=0, tiled=True),
        precision=lax.Precision.HIGHEST,
    )
    return running + jnp.einsum(
        "sp,prb->srb",
        partner_link,
        lax.all_gather(flipped, "pairs", axis=0, tiled=True),
        precision=lax.Precision.HIGHEST,
    )


def solution(mesh):
    placed = (P(None, "aux", "pairs"), P("aux", None, None), P(), P(), P(), P())
    return jax.shard_map(
        per_device, mesh=mesh, in_specs=placed, out_specs=P("pairs", "aux", None), check_vma=False
    )
```

profile of v0, /device:TPU:0, one launch (start us, length us, event | category | flops | bytes accessed | tf_op | source)
XLA Modules:
  0.0 141.3 jit_solution(13534873343749356057)
XLA Ops:
  6.5 1.6 %reshape.46 = bf16[4,2,2048]{2,1,0:T(2,128)(2,1)} reshape(bf16[8,32,64]{2,1,0:T(8,128)(2,1)} %param.8) | data formatting | bytes 65536
  8.1 5.2 %all-to-all-start = ((bf16[4,2,2048]{2,1,0:T(2,128)(2,1)}), bf16[4,2,2048]{2,1,0:T(2,128)(2,1)S(1)}, u32[]{:S(2)}, u32[]{:S(2)}) async-start(bf16[4,2,2048]{2,1,0:T(2,128)(2,1)} %reshape.46), calls=%async_computation | async-start | bytes 65536 | tf_op jit(solution)/shard_map/all_to_all | solution.py:44
  13.3 0.9 convert_reduce_fusion
  14.2 0.7 multiply_add_fusion
  14.8 3.2 %all-to-all-done = bf16[4,2,2048]{2,1,0:T(2,128)(2,1)S(1)} async-done(((bf16[4,2,2048]{2,1,0:T(2,128)(2,1)}), bf16[4,2,2048]{2,1,0:T(2,128)(2,1)S(1)}, u32[]{:S(2)}, u32[]{:S(2)}) %all-to-all-start) | async-done | bytes 32800 | tf_op jit(solution)/shard_map/all_to_all | solution.py:44
  18.2 0.1 all_to_all.29
  18.3 14.4 %all_gather.9 = bf16[2,256,256]{2,1,0:T(8,128)(2,1)S(1)} all-gather(bf16[2,32,256]{2,1,0:T(8,128)(2,1)S(1)} %all_to_all.29), channel_id=1, replica_groups=mesh['aux'=8,'pairs'=4] {'aux'}, dimensions={1}, use_global_device_ids=true | all-gather | bytes 294912 | tf_op jit(solution)/shard_map/all_gather | solution.py:8
  32.8 18.4 %while.10 = (s32[]{:T(128)}, f32[2,256,256]{2,0,1:T(2,128)S(1)}, bf16[2,256,256]{2,1,0:T(8,128)(2,1)S(1)}, bf16[28,256,256]{2,1,0:T(8,128)(2,1)}, s32[]{:T(128)}, /*index=5*/s32[]{:T(128)}) while((s32[]{:T(128)}, f32[2,256,256]{2,0,1:T(2,128)S(1)}, bf16[2,256,256]{2,1,0:T(8,128)(2,1)S(1)}, bf16[28,256,256]{2,1,0:T(8,128)(2,1)}, s32[]{:T(128)}, ...), condition=%wide.region_2.3_spmd, body=%wide.region_1.2_spmd.sunk | while | flops 1880883200 | bytes 8781909 | solution.py:18
  32.8 5.5 %fusion.36 = f32[1,256,256]{1,2,0:T(8,128)S(1)} fusion(bf16[28,256,256]{2,1,0:T(8,128)(2,1)} %get-tuple-element.76, bf16[2,256,256]{2,1,0:T(8,128)(2,1)S(1)} %get-tuple-element.75, s32[]{:T(128)S(6)} %copy.61), kind=kOutput, calls=%fused_computation.4.clone.1 | convolution fusion | flops 1880883200 | bytes 7733252 | tf_op jit(solution)/shard_map/while/body/eval_jaxpr/qac,qcb->ab/dot_general | solution.py:14
  38.3 0.2 copy.57
  38.4 3.5 %dynamic_update_slice.5 = f32[2,256,256]{2,0,1:T(2,128)S(1)} dynamic-update-slice(f32[2,256,256]{2,0,1:T(2,128)S(1)} %get-tuple-element.68, f32[1,256,256]{2,0,1:T(1,128)S(1)} %copy.57, s32[]{:T(128)S(6)} %copy.61, s32[]{:T(128)} %constant.17.clone.1..sunk, s32[]{:T(128)} %constant.17.clone.1..sunk) | dynamic-update-slice | bytes 524292 | tf_op jit(solution)/shard_map/while/body/jit(dynamic_update_index_in_dim)/dynamic_update_slice | solution.py:18
  42.0 5.5 %fusion.36 = f32[1,256,256]{1,2,0:T(8,128)S(1)} fusion(bf16[28,256,256]{2,1,0:T(8,128)(2,1)} %get-tuple-element.76, bf16[2,256,256]{2,1,0:T(8,128)(2,1)S(1)} %get-tuple-element.75, s32[]{:T(128)S(6)} %copy.61), kind=kOutput, calls=%fused_computation.4.clone.1 | convolution fusion | flops 1880883200 | bytes 7733252 | tf_op jit(solution)/shard_map/while/body/eval_jaxpr/qac,qcb->ab/dot_general | solution.py:14
  47.5 0.2 copy.57
  47.6 3.5 %dynamic_update_slice.5 = f32[2,256,256]{2,0,1:T(2,128)S(1)} dynamic-update-slice(f32[2,256,256]{2,0,1:T(2,128)S(1)} %get-tuple-element.68, f32[1,256,256]{2,0,1:T(1,128)S(1)} %copy.57, s32[]{:T(128)S(6)} %copy.61, s32[]{:T(128)} %constant.17.clone.1..sunk, s32[]{:T(128)} %constant.17.clone.1..sunk) | dynamic-update-slice | bytes 524292 | tf_op jit(solution)/shard_map/while/body/jit(dynamic_update_index_in_dim)/dynamic_update_slice | solution.py:18
  51.2 0.8 copy-done
  52.0 0.6 dynamic-slice
  53.5 54.1 %all-reduce.3.cloned.1.call-done = f32[2,256,256]{2,0,1:T(2,128)} async-done(((f32[2,256,256]{2,0,1:T(2,128)}), f32[2,256,256]{2,0,1:T(2,128)}) %all-reduce.3.cloned.1.call-update) | async-done | bytes 524304
  107.6 0.8 constant_dynamic-slice_fusion
  108.5 0.1 copy.42
  108.6 0.9 reshape.48
  109.6 3.4 %all-to-all-start.1 = ((f32[8,1,2048]{2,1,0:T(1,128)}), f32[8,1,2048]{2,1,0:T(1,128)S(1)}, u32[]{:S(2)}, u32[]{:S(2)}) async-start(f32[8,1,2048]{2,1,0:T(1,128)} %reshape.48), calls=%async_computation.1 | async-start | bytes 131072 | tf_op jit(solution)/shard_map/all_to_all | solution.py:27
  112.9 0.2 convolution_bitcast_fusion
  113.1 9.0 %all_gather.10 = f32[8,32,256]{2,1,0:T(8,128)S(1)} all-gather(f32[2,32,256]{2,1,0:T(8,128)S(1)} %copy_divide_fusion), channel_id=1, replica_groups=mesh['aux'=8,'pairs'=4] {'pairs'}, dimensions={0}, use_global_device_ids=true | all-gather | bytes 327680 | tf_op jit(solution)/shard_map/all_gather | solution.py:54
  122.1 0.5 broadcast.37
  122.6 0.8 reduce
  123.4 0.2 reshape.49
  123.6 0.2 copy.43
  123.8 0.1 all_to_all.33
  123.9 9.0 %all_gather.11 = f32[8,32,256]{2,1,0:T(8,128)S(1)} all-gather(f32[2,32,256]{2,1,0:T(8,128)S(1)} %bitcast.51), channel_id=1, replica_groups=mesh['aux'=8,'pairs'=4] {'pairs'}, dimensions={0}, use_global_device_ids=true | all-gather | bytes 327680 | tf_op jit(solution)/shard_map/all_gather | solution.py:60
  132.9 0.5 fusion.14
  133.4 0.4 convolution_add_fusion
  133.8 0.7 copy.45
  (20 shorter events, 0.5 us)
Async XLA Ops:
  8.1 9.9 %all-to-all-start = ((bf16[4,2,2048]{2,1,0:T(2,128)(2,1)}), bf16[4,2,2048]{2,1,0:T(2,128)(2,1)S(1)}, u32[]{:S(2)}, u32[]{:S(2)}) async-start(bf16[4,2,2048]{2,1,0:T(2,128)(2,1)} %reshape.46), calls=%async_computation | async-start | bytes 65536 | tf_op jit(solution)/shard_map/all_to_all | solution.py:44
  13.3 94.3 %all-reduce.3.cloned.1.call-start = ((), (), s32[]{:S(2)}) async-start(), calls=%async_computation.2 | async-start | bytes 1048576
  32.8 19.2 %copy-start.4 = (u32[32]{0:T(128)S(1)}, u32[32]{0:T(128)}, u32[]{:S(2)}) copy-start(u32[32]{0:T(128)} %constant.36) | copy-start | bytes 388
  32.8 20.5 %copy-start.2 = (f32[8]{0:T(128)S(1)}, f32[8]{0:T(128)}, u32[]{:S(2)}) copy-start(f32[8]{0:T(128)} %param.11) | copy-start | bytes 100
  32.8 20.6 %copy-start.1 = (f32[256]{0:T(256)S(1)}, f32[256]{0:T(256)}, u32[]{:S(2)}) copy-start(f32[256]{0:T(256)} %param.10) | copy-start | bytes 3076
  32.8 80.2 %copy-start.3 = (s32[8]{0:T(128)S(1)}, s32[8]{0:T(128)}, u32[]{:S(2)}) copy-start(s32[8]{0:T(128)} %param.13) | copy-start | bytes 100
  51.2 0.8 copy-start
  109.6 12.5 %all-to-all-start.1 = ((f32[8,1,2048]{2,1,0:T(1,128)}), f32[8,1,2048]{2,1,0:T(1,128)S(1)}, u32[]{:S(2)}, u32[]{:S(2)}) async-start(f32[8,1,2048]{2,1,0:T(1,128)} %reshape.48), calls=%async_computation.1 | async-start | bytes 131072 | tf_op jit(solution)/shard_map/all_to_all | solution.py:27
Sparse Core Ops, SparseCore 0:
  52.1 55.4 all-reduce.2
where the time goes:
time: 142 us; the launch traced here: 141 us
  waiting for transfers between devices  57.3 us (40%)
  blocking collectives  32.4 us (23%)
  local copies, waits for them, and re-layouts  14.4 us (10%)
  between operations  14.2 us (10%)
  matrix products  12 us (8%)
  starting transfers between devices  8.52 us (6%)
  other arithmetic  2.54 us (2%)
    unnamed x2, waiting for transfers between devices  54.1 us
    all_gather x1, blocking collectives, ladder_rows(): whole_tiles = lax.all_gather(amp_tiles, 'aux', axis=1, tiled=True)  14.4 us
    dot_general x2, matrix products, one_slot(): jnp.einsum('qac,qcb->ab', three_index, half_product, preferred_element_ty...  11 us
    all_gather x1, blocking collectives, per_device(): lax.all_gather(scaled, 'pairs', axis=0, tiled=True)  8.96 us
    all_gather x1, blocking collectives, per_device(): lax.all_gather(flipped, 'pairs', axis=0, tiled=True)  8.95 us
    dynamic_update_slice x4, local copies, waits for them, and re-layouts, ladder_rows(): running = lax.map(one_slot, whole_tiles)  7.36 us
    all_to_all x1, starting transfers between devices, per_device(): lax.all_to_all(amplitudes, 'pairs', split_axis=0, concat_axis=2, tiled=True)  5.16 us
    unnamed x16, local copies, waits for them, and re-layouts  5.06 us
  transfers between devices with their start and end apart: 3, of which 2 were waited for; matrix products, arithmetic and copies ran while one was open for 2% of the time, Pallas kernels for 0%

commit v1 on v0

v1 whole, which is shorter than its diff:
```python
import functools

import jax
import jax.numpy as jnp
from jax import lax
from jax.experimental import pallas as pl
from jax.experimental.pallas import tpu as pltpu
from jax.sharding import PartitionSpec as P

MESH = pl.DeviceIdType.MESH


def ladder_kernel(
    aux_size, groups,
    amp_ref, three_hbm, virt_ref, energy_ref, owner_ref, partner_ref,
    out_ref,
    three_buf, tiles, rows_all, sums, mate_in, z_out, z_in, gathered, virt_col,
    three_sem, tile_send, tile_recv, row_send, row_recv, fwd_send, fwd_recv,
    mate_send, mate_recv, z_send, z_recv, gat_send, gat_recv,
):
    pairs_all, rows, cols = amp_ref.shape
    naux, virt, _ = three_buf.shape
    per_group = pairs_all // groups
    chips = aux_size // 2
    capacity = out_ref.shape[0]
    me = lax.axis_index("aux")
    group = lax.axis_index("pairs")
    z, core = me // 2, lax.rem(me, 2)
    mate = z * 2 + (1 - core)

    def z_at(step):
        return lax.rem(z + step, chips)

    def group_at(step):
        return lax.rem(group + step, groups)

    load_three = pltpu.make_async_copy(three_hbm, three_buf, three_sem)
    load_three.start()

    barrier = pltpu.get_barrier_semaphore()
    pl.semaphore_signal(barrier, inc=1, device_id={"aux": mate, "pairs": group}, device_id_type=MESH)
    for k in range(1, chips):
        pl.semaphore_signal(
            barrier, inc=1, device_id={"aux": z_at(k) * 2 + core, "pairs": group}, device_id_type=MESH
        )
    for k in range(1, groups):
        pl.semaphore_signal(
            barrier, inc=1, device_id={"aux": me, "pairs": group_at(k)}, device_id_type=MESH
        )
    pl.semaphore_wait(barrier, 1 + (chips - 1) + (groups - 1))

    def to_mate(src, dst, send, recv):
        return pltpu.make_async_remote_copy(
            src_ref=src, dst_ref=dst, send_sem=send, recv_sem=recv,
            device_id={"aux": mate, "pairs": group}, device_id_type=MESH,
        )

    def to_chip(k, src, dst, send, recv):
        return pltpu.make_async_remote_copy(
            src_ref=src, dst_ref=dst, send_sem=send, recv_sem=recv,
            device_id={"aux": z_at(k) * 2 + core, "pairs": group}, device_id_type=MESH,
        )

    def to_group(k, src, dst, send, recv):
        return pltpu.make_async_remote_copy(
            src_ref=src, dst_ref=dst, send_sem=send, recv_sem=recv,
            device_id={"aux": me, "pairs": group_at(k)}, device_id_type=MESH,
        )

    tile_copies = [
        to_group(
            k, amp_ref.at[pl.ds(group_at(k) * per_group, per_group)], tiles.at[group],
            tile_send.at[k - 1], tile_recv.at[k - 1],
        )
        for k in range(1, groups)
    ]
    for copy in tile_copies:
        copy.start()
    tiles[group] = amp_ref[pl.ds(group * per_group, per_group)]
    virt_col[...] = jnp.transpose(jnp.broadcast_to(virt_ref[...], (128, virt)))
    for copy in tile_copies:
        copy.wait_recv()
    rows_all[me] = jnp.concatenate([tiles[j] for j in range(groups)], axis=-1)

    row_copies = [
        to_chip(k, rows_all.at[me], rows_all.at[me], row_send.at[k - 1], row_recv.at[k - 1])
        for k in range(1, chips)
    ]
    for copy in row_copies:
        copy.start()
    fwd_copies = []
    for k in range(chips):
        if k > 0:
            row_copies[k - 1].wait_recv()
        held = rows_all.at[z_at(chips - k) * 2 + core]
        copy = to_mate(held, held, fwd_send.at[k], fwd_recv.at[k])
        copy.start()
        fwd_copies.append(copy)
    load_three.wait()
    for copy in fwd_copies:
        copy.wait_recv()

    unroll = max(u for u in (1, 2, 3, 4) if naux % u == 0)
    trips = naux // unroll

    def ladder(p, first, last):
        def one(i, carry):
            amp = rows_all[:, p].reshape(virt, virt)
            lefts, halves = [], []
            for j in range(unroll):
                left = three_buf[i * unroll + j]
                half = lax.dot_general(
                    amp, left, (((1,), (1,)), ((), ())), preferred_element_type=jnp.float32
                )
                lefts.append(left)
                halves.append(half.astype(jnp.bfloat16))
            term = jnp.dot(
                jnp.concatenate(lefts, axis=1), jnp.concatenate(halves, axis=0),
                preferred_element_type=jnp.float32,
            )
            sums[p, 0] = sums[p, 0] + term.reshape(chips, 2, rows, virt)
            return carry

        lax.fori_loop(first, last, one, 0)

    def send_mate(p):
        whole = sums[p, 0].reshape(virt, virt)
        sums[p, 1] = jnp.transpose(whole).reshape(chips, 2, rows, virt)
        copy = to_mate(sums.at[p, :, :, 1 - core], mate_in.at[p], mate_send.at[p], mate_recv.at[p])
        copy.start()
        return copy

    def send_z(p, mate_copy):
        mate_copy.wait_recv()
        copies = []
        for k in range(1, chips):
            there = z_at(k)
            both = sums[p, :, there, core] + mate_in[p, :, there]
            z_out[p, k - 1] = both.astype(jnp.bfloat16)
            copy = to_chip(k, z_out.at[p, k - 1], z_in.at[p, k - 1], z_send.at[p, k - 1], z_recv.at[p, k - 1])
            copy.start()
            copies.append(copy)
        return copies

    def finish(p, z_copies):
        total = sums[p, :, z, core] + mate_in[p, :, z]
        for k, copy in enumerate(z_copies):
            copy.wait_recv()
            total = total + z_in[p, k].astype(jnp.float32)
        here = virt_col[pl.ds(me * rows, rows), 0:1]
        divisor = here + virt_ref[...] - energy_ref[group * per_group + p]
        mine = group * per_group + p
        gathered[mine] = (total / divisor[None]).astype(jnp.bfloat16)
        copies = []
        for k in range(1, groups):
            copy = to_group(
                k, gathered.at[mine], gathered.at[mine], gat_send.at[p, k - 1], gat_recv.at[p, k - 1]
            )
            copy.start()
            copies.append(copy)
        return copies

    sums[:, 0] = jnp.zeros((per_group, chips, 2, rows, virt), jnp.float32)
    mate_copies, z_copies, gat_copies = [], [], []
    for p in range(per_group):
        ladder(p, 0, trips // 2)
        if p > 0:
            z_copies.append(send_z(p - 1, mate_copies[p - 1]))
        ladder(p, trips // 2, trips)
        mate_copies.append(send_mate(p))
        if p > 0:
            gat_copies.append(finish(p - 1, z_copies[p - 1]))
    z_copies.append(send_z(per_group - 1, mate_copies[-1]))
    gat_copies.append(finish(per_group - 1, z_copies[-1]))

    count = jnp.int32(0)
    sources = [jnp.int32(0) for _ in range(capacity)]
    for p in range(pairs_all):
        held = owner_ref[p] == group
        sources = [
            jnp.where(jnp.logical_and(held, count == s), jnp.int32(p), src) for s, src in enumerate(sources)
        ]
        count = count + jnp.where(held, jnp.int32(1), jnp.int32(0))

    for copies in gat_copies:
        for copy in copies:
            copy.wait_recv()
    for s in range(capacity):
        other = partner_ref[sources[s]]
        block = gathered[sources[s]][0].astype(jnp.float32) + gathered[other][1].astype(jnp.float32)
        out_ref[s] = jnp.where(count > s, block, 0.0)

    for copy in tile_copies + row_copies + fwd_copies + mate_copies:
        copy.wait_send()
    for copies in z_copies + gat_copies:
        for copy in copies:
            copy.wait_send()


def per_device(aux_size, groups, amplitudes, three_index, virt_energy, pair_energy, owner, partner):
    pairs_all, rows, cols = amplitudes.shape
    naux, virt, _ = three_index.shape
    per_group = pairs_all // groups
    capacity = 2 * per_group
    chips = aux_size // 2
    dma = pltpu.SemaphoreType.DMA
    vmem = pl.BlockSpec(memory_space=pltpu.VMEM)
    smem = pl.BlockSpec(memory_space=pltpu.SMEM)
    return pl.pallas_call(
        functools.partial(ladder_kernel, aux_size, groups),
        out_shape=jax.ShapeDtypeStruct((capacity, rows, virt), jnp.float32),
        in_specs=[vmem, pl.BlockSpec(memory_space=pl.ANY), vmem, smem, smem, smem],
        out_specs=vmem,
        scratch_shapes=[
            pltpu.VMEM((naux, virt, virt), jnp.bfloat16),
            pltpu.VMEM((groups, per_group, rows, cols), jnp.bfloat16),
            pltpu.VMEM((aux_size, per_group, rows, virt), jnp.bfloat16),
            pltpu.VMEM((per_group, 2, chips, 2, rows, virt), jnp.float32),
            pltpu.VMEM((per_group, 2, chips, rows, virt), jnp.float32),
            pltpu.VMEM((per_group, chips - 1, 2, rows, virt), jnp.bfloat16),
            pltpu.VMEM((per_group, chips - 1, 2, rows, virt), jnp.bfloat16),
            pltpu.VMEM((pairs_all, 2, rows, virt), jnp.bfloat16),
            pltpu.VMEM((virt, 128), jnp.float32),
            dma,
            dma((groups - 1,)), dma((groups - 1,)),
            dma((chips - 1,)), dma((chips - 1,)),
            dma((chips,)), dma((chips,)),
            dma((per_group,)), dma((per_group,)),
            dma((per_group, chips - 1)), dma((per_group, chips - 1)),
            dma((per_group, groups - 1)), dma((per_group, groups - 1)),
        ],
        compiler_params=pltpu.CompilerParams(
            collective_id=0, has_side_effects=True, vmem_limit_bytes=40 * 1024 * 1024
        ),
        cost_estimate=pl.CostEstimate(
            flops=4 * per_group * naux * virt**3, bytes_accessed=2 * naux * virt**2, transcendentals=0
        ),
    )(amplitudes, three_index, virt_energy.reshape(1, virt), pair_energy, owner, partner)


def solution(mesh):
    placed = (P(None, "aux", "pairs"), P("aux", None, None), P(), P(), P(), P())
    return jax.shard_map(
        functools.partial(per_device, mesh.shape["aux"], mesh.shape["pairs"]),
        mesh=mesh, in_specs=placed, out_specs=P("pairs", "aux", None), check_vma=False,
    )
```

time: 142 us -> 41 us (0.29)
  waiting for transfers between devices: 57.3 us -> 0 us
  Pallas kernels: 0 us -> 34.5 us
  blocking collectives: 32.4 us -> 0 us
  between operations: 14.2 us -> 0.02 us
  matrix products: 12 us -> 0 us
  starting transfers between devices: 8.52 us -> 0 us
  local copies, waits for them, and re-layouts: 14.4 us -> 6.18 us
  other arithmetic: 2.54 us -> 0 us
    unnamed x2 -> x0, waiting for transfers between devices: 54.1 us -> none
    pallas_call x0 -> x1, Pallas kernels: none -> 34.5 us  [per_device(): pl.pallas_call(functools.partial(ladder_kernel, aux_size, groups), out_sh...]
    all_gather x3 -> x0, blocking collectives: 32.4 us -> none  [the longest x1 14.4 us: ladder_rows(): whole_tiles = lax.all_gather(amp_tiles, 'aux', axis=1, tiled=True)]
    dot_general x5 -> x0, matrix products: 12 us -> none  [the longest x2 11 us: one_slot(): jnp.einsum('qac,qcb->ab', three_index, half_product, preferred_element_ty...]
    all_to_all x2 -> x0, starting transfers between devices: 8.51 us -> none  [the longest x1 5.16 us: per_device(): lax.all_to_all(amplitudes, 'pairs', split_axis=0, concat_axis=2, tiled=True)]
    dynamic_update_slice x4 -> x0, local copies, waits for them, and re-layouts: 7.36 us -> none  [ladder_rows(): running = lax.map(one_slot, whole_tiles)]
    all_to_all x2 -> x0, waiting for transfers between devices: 3.18 us -> none  [the longest x1 3.18 us: per_device(): lax.all_to_all(amplitudes, 'pairs', split_axis=0, concat_axis=2, tiled=True)]
    unnamed x16 -> x13, local copies, waits for them, and re-layouts: 5.06 us -> 6.18 us
  transfers between devices with their start and end apart: 3 -> 0, of which waited for: 2 -> 0; matrix products, arithmetic and copies ran while one was open for 2% -> 0% of each run, Pallas kernels for 0% -> 0%
where the time goes in v1:
time: 41 us; the launch traced here: 40.7 us
  Pallas kernels  34.5 us (84%)
  local copies, waits for them, and re-layouts  6.18 us (15%)
    pallas_call x1, Pallas kernels, per_device(): pl.pallas_call(functools.partial(ladder_kernel, aux_size, groups), out_sh...  34.5 us
    unnamed x13, local copies, waits for them, and re-layouts  6.18 us

profile of v1, /device:TPU:0, one launch (start us, length us, event | category | flops | bytes accessed | tf_op | source)
XLA Modules:
  0.0 40.7 jit_solution(13572007623985299624)
XLA Ops:
  0.0 0.0 copy-start
  0.0 2.0 %copy-done = bf16[28,256,256]{2,1,0:T(8,128)(2,1)S(1)} copy-done((bf16[28,256,256]{2,1,0:T(8,128)(2,1)S(1)}, bf16[28,256,256]{2,1,0:T(8,128)(2,1)}, u32[]{:S(2)}) %copy-start) | copy-done | bytes 3670040
  2.0 0.0 copy-start.1
  2.0 0.8 %copy-done.1 = bf16[8,32,64]{2,1,0:T(8,128)(2,1)S(1)} copy-done((bf16[8,32,64]{2,1,0:T(8,128)(2,1)S(1)}, bf16[8,32,64]{2,1,0:T(8,128)(2,1)}, u32[]{:S(2)}) %copy-start.1) | copy-done | bytes 32792
  2.9 0.0 copy-start.2
  2.9 0.7 %copy-done.2 = f32[256]{0:T(256)S(1)} copy-done((f32[256]{0:T(256)S(1)}, f32[256]{0:T(256)}, u32[]{:S(2)}) %copy-start.2) | copy-done | bytes 1048
  3.6 0.0 copy-start.3
  3.6 0.7 %copy-done.3 = f32[8]{0:T(128)S(1)} copy-done((f32[8]{0:T(128)S(1)}, f32[8]{0:T(128)}, u32[]{:S(2)}) %copy-start.3) | copy-done | bytes 56
  4.2 0.0 copy-start.4
  4.2 0.7 %copy-done.4 = s32[8]{0:T(128)S(1)} copy-done((s32[8]{0:T(128)S(1)}, s32[8]{0:T(128)}, u32[]{:S(2)}) %copy-start.4) | copy-done | bytes 56
  4.9 0.0 copy-start.5
  4.9 0.7 %copy-done.5 = s32[8]{0:T(128)S(1)} copy-done((s32[8]{0:T(128)S(1)}, s32[8]{0:T(128)}, u32[]{:S(2)}) %copy-start.5) | copy-done | bytes 56
  5.5 34.5 %shard_map.64 = f32[4,32,256]{2,1,0:T(8,128)S(1)} custom-call(bf16[8,32,64]{2,1,0:T(8,128)(2,1)S(1)} %copy-done.1, bf16[28,256,256]{2,1,0:T(8,128)(2,1)S(1)} %copy-done, f32[1,256]{1,0:T(1,128)S(1)} %bitcast.1, f32[8]{0:T(128)S(1)} %copy-done.3, s32[8]{0:T(128)S(1)} %copy-done.4, s32[8]{0:T(128)S(1)} %copy-done.5), custom_call_target="tpu_custom_call" | custom-call | flops 3758096384 | bytes 3670016 | tf_op jit(solution)/shard_map/pallas_call | solution.py:209
  40.1 0.7 %copy.8 = f32[4,32,256]{2,1,0:T(8,128)} copy(f32[4,32,256]{2,1,0:T(8,128)S(1)} %shard_map.64) | data formatting | bytes 262144
Async XLA Ops:
  0.0 2.0 %copy-start = (bf16[28,256,256]{2,1,0:T(8,128)(2,1)S(1)}, bf16[28,256,256]{2,1,0:T(8,128)(2,1)}, u32[]{:S(2)}) copy-start(bf16[28,256,256]{2,1,0:T(8,128)(2,1)} %three_hbm.1) | copy-start | bytes 11010052
  2.0 0.8 %copy-start.1 = (bf16[8,32,64]{2,1,0:T(8,128)(2,1)S(1)}, bf16[8,32,64]{2,1,0:T(8,128)(2,1)}, u32[]{:S(2)}) copy-start(bf16[8,32,64]{2,1,0:T(8,128)(2,1)} %amp_ref.1) | copy-start | bytes 98308
  2.9 0.7 %copy-start.2 = (f32[256]{0:T(256)S(1)}, f32[256]{0:T(256)}, u32[]{:S(2)}) copy-start(f32[256]{0:T(256)} %param.8) | copy-start | bytes 3076
  3.6 0.7 %copy-start.3 = (f32[8]{0:T(128)S(1)}, f32[8]{0:T(128)}, u32[]{:S(2)}) copy-start(f32[8]{0:T(128)} %energy_ref.1) | copy-start | bytes 100
  4.2 0.7 %copy-start.4 = (s32[8]{0:T(128)S(1)}, s32[8]{0:T(128)}, u32[]{:S(2)}) copy-start(s32[8]{0:T(128)} %owner_ref.1) | copy-start | bytes 100
  4.9 0.7 %copy-start.5 = (s32[8]{0:T(128)S(1)}, s32[8]{0:T(128)}, u32[]{:S(2)}) copy-start(s32[8]{0:T(128)} %partner_ref.1) | copy-start | bytes 100

commit v2 on v1

--- a/solution.py
+++ b/solution.py
@@ -12,9 +12,9 @@
 
 def ladder_kernel(
     aux_size, groups,
-    amp_ref, three_hbm, virt_ref, energy_ref, owner_ref, partner_ref,
+    amp_ref, three_hbm, virt_hbm, energy_hbm, owner_hbm, partner_hbm,
     out_ref,
-    three_buf, tiles, rows_all, sums, mate_in, z_out, z_in, gathered, virt_col,
+    virt_ref, energy_ref, owner_ref, partner_ref, small_sem, own_sem, three_buf, tiles, rows_all, sums, mate_in, z_out, z_in, gathered, virt_col,
     three_sem, tile_send, tile_recv, row_send, row_recv, fwd_send, fwd_recv,
     mate_send, mate_recv, z_send, z_recv, gat_send, gat_recv,
 ):
@@ -36,6 +36,18 @@
 
     load_three = pltpu.make_async_copy(three_hbm, three_buf, three_sem)
     load_three.start()
+    own_tile = pltpu.make_async_copy(
+        amp_ref.at[pl.ds(group * per_group, per_group)], tiles.at[group], own_sem
+    )
+    own_tile.start()
+    small_loads = [
+        pltpu.make_async_copy(src, dst, small_sem.at[i])
+        for i, (src, dst) in enumerate(
+            [(virt_hbm, virt_ref), (energy_hbm, energy_ref), (owner_hbm, owner_ref), (partner_hbm, partner_ref)]
+        )
+    ]
+    for load in small_loads:
+        load.start()
 
     barrier = pltpu.get_barrier_semaphore()
     pl.semaphore_signal(barrier, inc=1, device_id={"aux": mate, "pairs": group}, device_id_type=MESH)
@@ -76,8 +88,10 @@
     ]
     for copy in tile_copies:
         copy.start()
-    tiles[group] = amp_ref[pl.ds(group * per_group, per_group)]
+    for load in small_loads:
+        load.wait()
     virt_col[...] = jnp.transpose(jnp.broadcast_to(virt_ref[...], (128, virt)))
+    own_tile.wait()
     for copy in tile_copies:
         copy.wait_recv()
     rows_all[me] = jnp.concatenate([tiles[j] for j in range(groups)], axis=-1)
@@ -205,13 +219,19 @@
     chips = aux_size // 2
     dma = pltpu.SemaphoreType.DMA
     vmem = pl.BlockSpec(memory_space=pltpu.VMEM)
-    smem = pl.BlockSpec(memory_space=pltpu.SMEM)
+    hbm = pl.BlockSpec(memory_space=pltpu.HBM)
     return pl.pallas_call(
         functools.partial(ladder_kernel, aux_size, groups),
         out_shape=jax.ShapeDtypeStruct((capacity, rows, virt), jnp.float32),
-        in_specs=[vmem, pl.BlockSpec(memory_space=pl.ANY), vmem, smem, smem, smem],
+        in_specs=[hbm] * 6,
         out_specs=vmem,
         scratch_shapes=[
+            pltpu.VMEM((1, virt), jnp.float32),
+            pltpu.SMEM((pairs_all,), jnp.float32),
+            pltpu.SMEM((pairs_all,), jnp.int32),
+            pltpu.SMEM((pairs_all,), jnp.int32),
+            dma((4,)),
+            dma,
             pltpu.VMEM((naux, virt, virt), jnp.bfloat16),
             pltpu.VMEM((groups, per_group, rows, cols), jnp.bfloat16),
             pltpu.VMEM((aux_size, per_group, rows, virt), jnp.bfloat16),
@@ -230,7 +250,7 @@
             dma((per_group, groups - 1)), dma((per_group, groups - 1)),
         ],
         compiler_params=pltpu.CompilerParams(
-            collective_id=0, has_side_effects=True, vmem_limit_bytes=40 * 1024 * 1024
+            collective_id=0, has_side_effects=True, vmem_limit_bytes=60 * 1024 * 1024
         ),
         cost_estimate=pl.CostEstimate(
             flops=4 * per_group * naux * virt**3, bytes_accessed=2 * naux * virt**2, transcendentals=0

time: 41 us -> 36.4 us (0.89)
  local copies, waits for them, and re-layouts: 6.18 us -> 1.57 us
    unnamed x13 -> x1, local copies, waits for them, and re-layouts: 6.18 us -> 1.57 us
where the time goes in v2:
time: 36.4 us; the launch traced here: 36.2 us
  Pallas kernels  34.6 us (95%)
  local copies, waits for them, and re-layouts  1.57 us (4%)
    pallas_call x1, Pallas kernels, per_device(): pl.pallas_call(functools.partial(ladder_kernel, aux_size, groups), out_sh...  34.6 us
    unnamed x1, local copies, waits for them, and re-layouts  1.57 us

profile of v2, /device:TPU:0, one launch (start us, length us, event | category | flops | bytes accessed | tf_op | source)
XLA Modules:
  0.0 36.2 jit_solution(7288318689697508751)
XLA Ops:
  0.0 34.6 %shard_map.64 = f32[4,32,256]{2,1,0:T(8,128)} custom-call(bf16[8,32,64]{2,1,0:T(8,128)(2,1)} %amp_ref.1, bf16[28,256,256]{2,1,0:T(8,128)(2,1)} %three_hbm.1, f32[1,256]{1,0:T(1,128)} %bitcast.1, f32[8]{0:T(128)} %energy_hbm.1, s32[8]{0:T(128)} %owner_hbm.1, s32[8]{0:T(128)} %partner_hbm.1), custom_call_target="tpu_custom_call" | custom-call | flops 3758096384 | bytes 3670016 | tf_op jit(solution)/shard_map/pallas_call | solution.py:223
  34.6 1.6 %copy.8 = f32[4,32,256]{2,1,0:T(8,128)} copy(f32[4,32,256]{2,1,0:T(8,128)} %shard_map.64) | data formatting | bytes 262144

commit v3 on v2

--- a/solution.py
+++ b/solution.py
@@ -14,7 +14,7 @@
     aux_size, groups,
     amp_ref, three_hbm, virt_hbm, energy_hbm, owner_hbm, partner_hbm,
     out_ref,
-    virt_ref, energy_ref, owner_ref, partner_ref, small_sem, own_sem, three_buf, tiles, rows_all, sums, mate_in, z_out, z_in, gathered, virt_col,
+    virt_ref, energy_ref, owner_ref, partner_ref, small_sem, own_sem, amp_buf, packed, three_buf, tiles, rows_all, sums, mate_in, z_out, z_in, gathered, virt_col,
     three_sem, tile_send, tile_recv, row_send, row_recv, fwd_send, fwd_recv,
     mate_send, mate_recv, z_send, z_recv, gat_send, gat_recv,
 ):
@@ -34,12 +34,10 @@
     def group_at(step):
         return lax.rem(group + step, groups)
 
+    load_amp = pltpu.make_async_copy(amp_ref, amp_buf, own_sem)
+    load_amp.start()
     load_three = pltpu.make_async_copy(three_hbm, three_buf, three_sem)
     load_three.start()
-    own_tile = pltpu.make_async_copy(
-        amp_ref.at[pl.ds(group * per_group, per_group)], tiles.at[group], own_sem
-    )
-    own_tile.start()
     small_loads = [
         pltpu.make_async_copy(src, dst, small_sem.at[i])
         for i, (src, dst) in enumerate(
@@ -59,6 +57,10 @@
         pl.semaphore_signal(
             barrier, inc=1, device_id={"aux": me, "pairs": group_at(k)}, device_id_type=MESH
         )
+    load_amp.wait()
+    for j in range(groups):
+        packed[j] = jnp.concatenate([amp_buf[j * per_group + q] for q in range(per_group)], axis=-1)
+    tiles[group] = packed[group]
     pl.semaphore_wait(barrier, 1 + (chips - 1) + (groups - 1))
 
     def to_mate(src, dst, send, recv):
@@ -81,7 +83,7 @@
 
     tile_copies = [
         to_group(
-            k, amp_ref.at[pl.ds(group_at(k) * per_group, per_group)], tiles.at[group],
+            k, packed.at[group_at(k)], tiles.at[group],
             tile_send.at[k - 1], tile_recv.at[k - 1],
         )
         for k in range(1, groups)
@@ -91,10 +93,12 @@
     for load in small_loads:
         load.wait()
     virt_col[...] = jnp.transpose(jnp.broadcast_to(virt_ref[...], (128, virt)))
-    own_tile.wait()
     for copy in tile_copies:
         copy.wait_recv()
-    rows_all[me] = jnp.concatenate([tiles[j] for j in range(groups)], axis=-1)
+    for q in range(per_group):
+        rows_all[me, q] = jnp.concatenate(
+            [tiles[j][:, q * cols : (q + 1) * cols] for j in range(groups)], axis=-1
+        )
 
     row_copies = [
         to_chip(k, rows_all.at[me], rows_all.at[me], row_send.at[k - 1], row_recv.at[k - 1])
@@ -114,7 +118,7 @@
     for copy in fwd_copies:
         copy.wait_recv()
 
-    unroll = max(u for u in (1, 2, 3, 4) if naux % u == 0)
+    unroll = max(u for u in range(1, 15) if naux % u == 0)
     trips = naux // unroll
 
     def ladder(p, first, last):
@@ -222,7 +226,7 @@
     hbm = pl.BlockSpec(memory_space=pltpu.HBM)
     return pl.pallas_call(
         functools.partial(ladder_kernel, aux_size, groups),
-        out_shape=jax.ShapeDtypeStruct((capacity, rows, virt), jnp.float32),
+        out_shape=pltpu.VMEM((capacity, rows, virt), jnp.float32),
         in_specs=[hbm] * 6,
         out_specs=vmem,
         scratch_shapes=[
@@ -232,8 +236,10 @@
             pltpu.SMEM((pairs_all,), jnp.int32),
             dma((4,)),
             dma,
+            pltpu.VMEM(amplitudes.shape, jnp.bfloat16),
+            pltpu.VMEM((groups, rows, per_group * cols), jnp.bfloat16),
             pltpu.VMEM((naux, virt, virt), jnp.bfloat16),
-            pltpu.VMEM((groups, per_group, rows, cols), jnp.bfloat16),
+            pltpu.VMEM((groups, rows, per_group * cols), jnp.bfloat16),
             pltpu.VMEM((aux_size, per_group, rows, virt), jnp.bfloat16),
             pltpu.VMEM((per_group, 2, chips, 2, rows, virt), jnp.float32),
             pltpu.VMEM((per_group, 2, chips, rows, virt), jnp.float32),

time: 36.4 us -> 31.6 us (0.87)
  Pallas kernels: 34.6 us -> 30.8 us
  local copies, waits for them, and re-layouts: 1.57 us -> 0.66 us
    pallas_call x1, Pallas kernels: 34.6 us -> 30.8 us  [per_device(): pl.pallas_call(functools.partial(ladder_kernel, aux_size, groups), out_sh...]
    unnamed x1, local copies, waits for them, and re-layouts: 1.57 us -> 0.66 us
where the time goes in v3:
time: 31.6 us; the launch traced here: 31.5 us
  Pallas kernels  30.8 us (97%)
  local copies, waits for them, and re-layouts  0.66 us (2%)
    pallas_call x1, Pallas kernels, per_device(): pl.pallas_call(functools.partial(ladder_kernel, aux_size, groups), out_sh...  30.8 us
    unnamed x1, local copies, waits for them, and re-layouts  0.66 us

profile of v3, /device:TPU:0, one launch (start us, length us, event | category | flops | bytes accessed | tf_op | source)
XLA Modules:
  0.0 31.5 jit_solution(475016808360662273)
XLA Ops:
  0.0 30.8 %shard_map.64 = f32[4,32,256]{2,1,0:T(8,128)S(1)} custom-call(bf16[8,32,64]{2,1,0:T(8,128)(2,1)} %amp_ref.1, bf16[28,256,256]{2,1,0:T(8,128)(2,1)} %three_hbm.1, f32[1,256]{1,0:T(1,128)} %bitcast.1, f32[8]{0:T(128)} %energy_hbm.1, s32[8]{0:T(128)} %owner_hbm.1, s32[8]{0:T(128)} %partner_hbm.1), custom_call_target="tpu_custom_call" | custom-call | flops 3758096384 | bytes 3670016 | tf_op jit(solution)/shard_map/pallas_call | solution.py:227
  30.8 0.7 %copy.8 = f32[4,32,256]{2,1,0:T(8,128)} copy(f32[4,32,256]{2,1,0:T(8,128)S(1)} %shard_map.64) | data formatting | bytes 262144

commit v4 on v3

--- a/solution.py
+++ b/solution.py
@@ -15,7 +15,7 @@
     amp_ref, three_hbm, virt_hbm, energy_hbm, owner_hbm, partner_hbm,
     out_ref,
     virt_ref, energy_ref, owner_ref, partner_ref, small_sem, own_sem, amp_buf, packed, three_buf, tiles, rows_all, sums, mate_in, z_out, z_in, gathered, virt_col,
-    three_sem, tile_send, tile_recv, row_send, row_recv, fwd_send, fwd_recv,
+    three_sem, tile_send, tile_recv, fwd_send, fwd_recv,
     mate_send, mate_recv, z_send, z_recv, gat_send, gat_recv,
 ):
     pairs_all, rows, cols = amp_ref.shape
@@ -49,19 +49,17 @@
 
     barrier = pltpu.get_barrier_semaphore()
     pl.semaphore_signal(barrier, inc=1, device_id={"aux": mate, "pairs": group}, device_id_type=MESH)
-    for k in range(1, chips):
+    others = [(k, m) for k in range(chips) for m in range(groups) if k or m]
+    for k, m in others:
         pl.semaphore_signal(
-            barrier, inc=1, device_id={"aux": z_at(k) * 2 + core, "pairs": group}, device_id_type=MESH
-        )
-    for k in range(1, groups):
-        pl.semaphore_signal(
-            barrier, inc=1, device_id={"aux": me, "pairs": group_at(k)}, device_id_type=MESH
-        )
+            barrier, inc=1, device_id={"aux": z_at(k) * 2 + core, "pairs": group_at(m)}, device_id_type=MESH
+        )
+
     load_amp.wait()
     for j in range(groups):
         packed[j] = jnp.concatenate([amp_buf[j * per_group + q] for q in range(per_group)], axis=-1)
-    tiles[group] = packed[group]
-    pl.semaphore_wait(barrier, 1 + (chips - 1) + (groups - 1))
+    tiles[me, group] = packed[group]
+    pl.semaphore_wait(barrier, 1 + len(others))
 
     def to_mate(src, dst, send, recv):
         return pltpu.make_async_remote_copy(
@@ -81,48 +79,43 @@
             device_id={"aux": me, "pairs": group_at(k)}, device_id_type=MESH,
         )
 
-    tile_copies = [
-        to_group(
-            k, packed.at[group_at(k)], tiles.at[group],
-            tile_send.at[k - 1], tile_recv.at[k - 1],
-        )
-        for k in range(1, groups)
-    ]
-    for copy in tile_copies:
+    tile_copies = {
+        (k, m): pltpu.make_async_remote_copy(
+            src_ref=packed.at[group_at(m)], dst_ref=tiles.at[me, group],
+            send_sem=tile_send.at[k, m], recv_sem=tile_recv.at[k, m],
+            device_id={"aux": z_at(k) * 2 + core, "pairs": group_at(m)}, device_id_type=MESH,
+        )
+        for k, m in others
+    }
+    for copy in tile_copies.values():
         copy.start()
     for load in small_loads:
         load.wait()
     virt_col[...] = jnp.transpose(jnp.broadcast_to(virt_ref[...], (128, virt)))
-    for copy in tile_copies:
-        copy.wait_recv()
-    for q in range(per_group):
-        rows_all[me, q] = jnp.concatenate(
-            [tiles[j][:, q * cols : (q + 1) * cols] for j in range(groups)], axis=-1
-        )
-
-    row_copies = [
-        to_chip(k, rows_all.at[me], rows_all.at[me], row_send.at[k - 1], row_recv.at[k - 1])
-        for k in range(1, chips)
-    ]
-    for copy in row_copies:
-        copy.start()
+
     fwd_copies = []
     for k in range(chips):
-        if k > 0:
-            row_copies[k - 1].wait_recv()
-        held = rows_all.at[z_at(chips - k) * 2 + core]
+        for m in range(groups):
+            if k or m:
+                tile_copies[k, m].wait_recv()
+        held = tiles.at[z_at(chips - k) * 2 + core]
         copy = to_mate(held, held, fwd_send.at[k], fwd_recv.at[k])
         copy.start()
         fwd_copies.append(copy)
     load_three.wait()
     for copy in fwd_copies:
         copy.wait_recv()
+    for a in range(aux_size):
+        for q in range(per_group):
+            rows_all[a, q] = jnp.concatenate(
+                [tiles[a, j][:, q * cols : (q + 1) * cols] for j in range(groups)], axis=-1
+            )
 
     unroll = max(u for u in range(1, 15) if naux % u == 0)
     trips = naux // unroll
 
     def ladder(p, first, last):
-        def one(i, carry):
+        def one(i, carry, fresh=False):
             amp = rows_all[:, p].reshape(virt, virt)
             lefts, halves = [], []
             for j in range(unroll):
@@ -136,9 +129,13 @@
                 jnp.concatenate(lefts, axis=1), jnp.concatenate(halves, axis=0),
                 preferred_element_type=jnp.float32,
             )
-            sums[p, 0] = sums[p, 0] + term.reshape(chips, 2, rows, virt)
+            term = term.reshape(chips, 2, rows, virt)
+            sums[p, 0] = term if fresh else sums[p, 0] + term
             return carry
 
+        if first == 0 and last > 0:
+            first = 1
+            one(0, 0, fresh=True)
         lax.fori_loop(first, last, one, 0)
 
     def send_mate(p):
@@ -178,7 +175,6 @@
             copies.append(copy)
         return copies
 
-    sums[:, 0] = jnp.zeros((per_group, chips, 2, rows, virt), jnp.float32)
     mate_copies, z_copies, gat_copies = [], [], []
     for p in range(per_group):
         ladder(p, 0, trips // 2)
@@ -208,7 +204,7 @@
         block = gathered[sources[s]][0].astype(jnp.float32) + gathered[other][1].astype(jnp.float32)
         out_ref[s] = jnp.where(count > s, block, 0.0)
 
-    for copy in tile_copies + row_copies + fwd_copies + mate_copies:
+    for copy in list(tile_copies.values()) + fwd_copies + mate_copies:
         copy.wait_send()
     for copies in z_copies + gat_copies:
         for copy in copies:
@@ -239,7 +235,7 @@
             pltpu.VMEM(amplitudes.shape, jnp.bfloat16),
             pltpu.VMEM((groups, rows, per_group * cols), jnp.bfloat16),
             pltpu.VMEM((naux, virt, virt), jnp.bfloat16),
-            pltpu.VMEM((groups, rows, per_group * cols), jnp.bfloat16),
+            pltpu.VMEM((aux_size, groups, rows, per_group * cols), jnp.bfloat16),
             pltpu.VMEM((aux_size, per_group, rows, virt), jnp.bfloat16),
             pltpu.VMEM((per_group, 2, chips, 2, rows, virt), jnp.float32),
             pltpu.VMEM((per_group, 2, chips, rows, virt), jnp.float32),
@@ -248,8 +244,7 @@
             pltpu.VMEM((pairs_all, 2, rows, virt), jnp.bfloat16),
             pltpu.VMEM((virt, 128), jnp.float32),
             dma,
-            dma((groups - 1,)), dma((groups - 1,)),
-            dma((chips - 1,)), dma((chips - 1,)),
+            dma((chips, groups)), dma((chips, groups)),
             dma((chips,)), dma((chips,)),
             dma((per_group,)), dma((per_group,)),
             dma((per_group, chips - 1)), dma((per_group, chips - 1)),

time: 31.6 us -> 30.9 us (0.978)
  Pallas kernels: 30.8 us -> 30.1 us
    pallas_call x1, Pallas kernels: 30.8 us -> 30.1 us  [per_device(): pl.pallas_call(functools.partial(ladder_kernel, aux_size, groups), out_sh...]
where the time goes in v4:
time: 30.9 us; the launch traced here: 30.8 us
  Pallas kernels  30.1 us (97%)
  local copies, waits for them, and re-layouts  0.66 us (2%)
    pallas_call x1, Pallas kernels, per_device(): pl.pallas_call(functools.partial(ladder_kernel, aux_size, groups), out_sh...  30.1 us
    unnamed x1, local copies, waits for them, and re-layouts  0.66 us

profile of v4, /device:TPU:0, one launch (start us, length us, event | category | flops | bytes accessed | tf_op | source)
XLA Modules:
  0.0 30.8 jit_solution(15652589806844820407)
XLA Ops:
  0.0 30.1 %shard_map.64 = f32[4,32,256]{2,1,0:T(8,128)S(1)} custom-call(bf16[8,32,64]{2,1,0:T(8,128)(2,1)} %amp_ref.1, bf16[28,256,256]{2,1,0:T(8,128)(2,1)} %three_hbm.1, f32[1,256]{1,0:T(1,128)} %bitcast.1, f32[8]{0:T(128)} %energy_hbm.1, s32[8]{0:T(128)} %owner_hbm.1, s32[8]{0:T(128)} %partner_hbm.1), custom_call_target="tpu_custom_call" | custom-call | flops 3758096384 | bytes 3670016 | tf_op jit(solution)/shard_map/pallas_call | solution.py:223
  30.1 0.7 %copy.8 = f32[4,32,256]{2,1,0:T(8,128)} copy(f32[4,32,256]{2,1,0:T(8,128)S(1)} %shard_map.64) | data formatting | bytes 262144
